TPU v7x, 32 devices: a whole 2x2x4 slice. The times are simulated.
32 devices in a mesh: seq: 8 (over z, x), grp: 4 (over y, core).
Axes of the slice: x: 2, y: 2, z: 4, core: 2. Of those that a mesh axis runs over, the one named last changes fastest.
Arguments:
- queries: bfloat16 [4, 128, 4096], P('grp', 'seq'), may hold values from -200 to 200
- prefix_keys: bfloat16 [4, 8192, 512], P('grp', 'seq'), may hold values from -20 to 20
- prefix_values: bfloat16 [4, 8192, 512], P('grp', 'seq'), may hold values from -6 to 6
- suffix_keys: bfloat16 [4, 128, 512], P('grp', 'seq'), may hold values from -48 to 48
- suffix_values: bfloat16 [4, 128, 512], P('grp', 'seq'), may hold values from -6 to 6
- parents: int32 [4, 128], P('grp'), may hold values from 0 to 127, as said below
- out_proj: bfloat16 [4096, 4096], P('seq'), may hold values from -0.09375 to 0.09375
- residual: bfloat16 [4, 128, 4096], P('grp', 'seq'), may hold values from -6 to 6
- norm_gain: float32 [4096], replicated, may hold values from 0.5 to 1.5
- router: bfloat16 [4096, 32], replicated, may hold values from -0.09375 to 0.09375
- routes: int32 [4, 128, 8], P('grp', 'seq'), may hold values from 0 to 31, all different within a row; in each aligned block of 16 rows (0 to 15, 16 to 31, ..., all dimensions but the last counted through in order) at most 8 rows name the same one
- expert_gate: bfloat16 [32, 4096, 768], P(('seq', 'grp')), may hold values from -0.09375 to 0.09375
- expert_up: bfloat16 [32, 4096, 768], P(('seq', 'grp')), may hold values from -0.09375 to 0.09375
- expert_down: bfloat16 [32, 768, 4096], P(('seq', 'grp')), may hold values from -0.21875 to 0.21875
Outputs:
- layer_out: bfloat16 [4, 128, 4096], P('grp', 'seq')
Inputs may be any that keep to these rules, and one draw needn't show every extreme that they name: Each request's rows form a forest of 8 levels, each a run of 16 rows: rows of the first level are their own parents; any other row's parent is a row of the level just before its own. `routes`: among the rows of one device no expert is named more than 8 times.
All inputs are finite; a program needn't handle non-finite values.
Results may differ from a plain program's by a relative error of at most 0.012.
Values may be sent and summed in bfloat16 or wider, within the bound.
A program may use at most 128 MiB of HBM per device.

v0:
```python
import jax
import jax.numpy as jnp
from jax import lax
from jax.sharding import PartitionSpec as P

HEADS = 32
KVH = 4
HD = 128
DEPTH = 8


EPSILON = 1e-06


def visible_mask(parent_row):
    count = parent_row.shape[0]
    positions = jnp.arange(count, dtype=jnp.int32)
    current = positions
    visible = current[:, None] == positions[None, :]
    for level in range(DEPTH - 1):
        current = parent_row[current]
        visible = visible | (current[:, None] == positions[None, :])
    return visible


def local(
    queries,
    prefix_keys,
    prefix_values,
    suffix_keys,
    suffix_values,
    parents,
    out_proj,
    residual,
    norm_gain,
    router,
    routes,
    expert_gate,
    expert_up,
    expert_down,
):
    seq_count = lax.axis_size("seq")
    seq_index = lax.axis_index("seq")
    query_local = queries[0]
    rows_local = query_local.shape[0]
    all_queries = lax.all_gather(query_local, "seq", axis=0, tiled=True)
    total_rows = all_queries.shape[0]
    group = HEADS // KVH
    scale = HD ** (-0.5)
    key_local = prefix_keys[0]
    value_local = prefix_values[0]
    maxima = []
    totals = []
    partials = []
    for head_kv in range(KVH):
        query_block = all_queries[:, head_kv * group * HD : (head_kv + 1) * group * HD].reshape(
            total_rows, group, HD
        )
        key_block = key_local[:, head_kv * HD : (head_kv + 1) * HD]
        value_block = value_local[:, head_kv * HD : (head_kv + 1) * HD]
        scores = (
            jnp.einsum("rgd,kd->rgk", query_block, key_block, preferred_element_type=jnp.float32)
            * scale
        )
        block_max = jnp.max(scores, axis=2)
        weights = jnp.exp(scores - block_max[:, :, None])
        totals.append(jnp.sum(weights, axis=2))
        partials.append(
            jnp.einsum(
                "rgk,kd->rgd",
                weights.astype(jnp.bfloat16),
                value_block,
                preferred_element_type=jnp.float32,
            )
        )
        maxima.append(block_max)
    local_max = jnp.concatenate(maxima, axis=1)
    local_total = jnp.concatenate(totals, axis=1)
    local_out = jnp.concatenate(partials, axis=1).reshape(total_rows, HEADS * HD)
    own_heads = HEADS // seq_count
    head_start = seq_index * own_heads
    whole_max = lax.pmax(local_max.astype(jnp.bfloat16), "seq").astype(local_max.dtype)
    factor = jnp.exp(local_max - whole_max)
    scaled_out = (local_out.reshape(total_rows, HEADS, HD) * factor[:, :, None]).reshape(
        total_rows, HEADS * HD
    )
    prefix_total, prefix_out = (
        lax.psum_scatter(
            (local_total * factor).astype(jnp.bfloat16), "seq", scatter_dimension=1, tiled=True
        ).astype(jnp.float32),
        lax.psum_scatter(
            scaled_out.astype(jnp.bfloat16), "seq", scatter_dimension=1, tiled=True
        ).astype(jnp.float32),
    )
    prefix_max = lax.dynamic_slice_in_dim(whole_max, head_start, own_heads, 1)
    suffix_all_keys, suffix_all_values = (
        lax.all_gather(suffix_keys[0], "seq", axis=0, tiled=True),
        lax.all_gather(suffix_values[0], "seq", axis=0, tiled=True),
    )
    kv_index = head_start // group
    key_suffix = lax.dynamic_slice_in_dim(suffix_all_keys, kv_index * HD, HD, 1)
    value_suffix = lax.dynamic_slice_in_dim(suffix_all_values, kv_index * HD, HD, 1)
    own_queries = lax.dynamic_slice_in_dim(all_queries, head_start * HD, own_heads * HD, 1).reshape(
        total_rows, own_heads, HD
    )
    visible = visible_mask(parents[0])
    suffix_scores = (
        jnp.einsum("rhd,jd->rhj", own_queries, key_suffix, preferred_element_type=jnp.float32)
        * scale
    )
    suffix_scores = jnp.where(visible[:, None, :], suffix_scores, -jnp.inf)
    joint_max = jnp.maximum(prefix_max, jnp.max(suffix_scores, axis=2))
    prefix_factor = jnp.exp(prefix_max - joint_max)
    suffix_weights = jnp.exp(suffix_scores - joint_max[:, :, None])
    joint_total = prefix_total * prefix_factor + jnp.sum(suffix_weights, axis=2)
    suffix_out = jnp.einsum(
        "rhj,jd->rhd",
        suffix_weights.astype(jnp.bfloat16),
        value_suffix,
        preferred_element_type=jnp.float32,
    )
    joint_out = (
        prefix_out.reshape(total_rows, own_heads, HD) * prefix_factor[:, :, None] + suffix_out
    )
    attention = (
        (joint_out / joint_total[:, :, None])
        .astype(jnp.bfloat16)
        .reshape(total_rows, own_heads * HD)
    )
    projected = lax.psum_scatter(
        jnp.dot(attention, out_proj, preferred_element_type=jnp.float32).astype(jnp.bfloat16),
        "seq",
        scatter_dimension=0,
        tiled=True,
    ).astype(jnp.float32)
    mixed = residual[0].astype(jnp.float32) + projected
    inverse = lax.rsqrt(jnp.mean(mixed * mixed, axis=1, keepdims=True) + EPSILON)
    normed = (mixed * inverse * norm_gain[None, :]).astype(jnp.bfloat16)
    logits = jnp.dot(normed, router, preferred_element_type=jnp.float32)
    experts = router.shape[1]
    expert_ids = jnp.arange(experts, dtype=jnp.int32)
    chosen_ids = routes[0]
    top = chosen_ids.shape[1]
    matches = chosen_ids[:, :, None] == expert_ids[None, None, :]
    chosen = jnp.sum(jnp.where(matches, logits[:, None, :], 0.0), axis=2)
    sig = jax.nn.sigmoid(chosen)
    gates = sig / jnp.sum(sig, axis=1, keepdims=True)
    devices = lax.axis_size("seq") * lax.axis_size("grp")
    capacity = max(2, 2 * rows_local * top // devices)
    flat_ids = chosen_ids.reshape(-1)
    one_hot = (flat_ids[:, None] == expert_ids[None, :]).astype(jnp.int32)
    slots = jnp.sum(jnp.cumsum(one_hot, axis=0) * one_hot, axis=1) - 1
    position = flat_ids * capacity + slots
    slot_index = jnp.arange(experts * capacity, dtype=jnp.int32)
    selector = (slot_index[:, None] == position[None, :]).reshape(
        experts * capacity, rows_local, top
    )
    dispatch_rows = jnp.sum(selector.astype(jnp.int32), axis=2).astype(jnp.bfloat16)
    model_width = normed.shape[1]
    outgoing = (
        jnp.dot(dispatch_rows, normed, preferred_element_type=jnp.float32)
        .astype(jnp.bfloat16)
        .reshape(experts, capacity, model_width)
    )
    gate_weight = expert_gate[0]
    up_weight = expert_up[0]
    down_weight = expert_down[0]
    arrived = lax.all_to_all(outgoing, ("seq", "grp"), split_axis=0, concat_axis=0, tiled=True)
    flat = arrived.reshape(-1, model_width)
    gate_part = jnp.dot(flat, gate_weight, preferred_element_type=jnp.float32)
    up_part = jnp.dot(flat, up_weight, preferred_element_type=jnp.float32)
    act = (jax.nn.silu(gate_part) * up_part).astype(jnp.bfloat16)
    returned = lax.all_to_all(
        jnp.dot(act, down_weight, preferred_element_type=jnp.float32)
        .astype(jnp.bfloat16)
        .reshape(arrived.shape),
        ("seq", "grp"),
        split_axis=0,
        concat_axis=0,
        tiled=True,
    ).reshape(experts * capacity, model_width)
    picked = returned[position].reshape(rows_local, top, model_width)
    moe = jnp.sum(picked.astype(jnp.float32) * gates[:, :, None], axis=1)
    return (mixed + moe).astype(jnp.bfloat16)[None]


def solution(mesh):
    in_specs = (
        P("grp", "seq", None),
        P("grp", "seq", None),
        P("grp", "seq", None),
        P("grp", "seq", None),
        P("grp", "seq", None),
        P("grp", None),
        P("seq", None),
        P("grp", "seq", None),
        P(),
        P(),
        P("grp", "seq", None),
        P(("seq", "grp"), None, None),
        P(("seq", "grp"), None, None),
        P(("seq", "grp"), None, None),
    )
    out_specs = P("grp", "seq", None)
    return jax.shard_map(local, mesh=mesh, in_specs=in_specs, out_specs=out_specs, check_vma=False)
```

profile of v0, /device:TPU:0, one launch (start us, length us, event | category | flops | bytes accessed | tf_op | source)
XLA Modules:
  0.0 374.0 jit_solution(12606351752294740407)
XLA Ops:
  7.3 1.7 gather_fusion
  9.0 1.6 gather_fusion.1
  10.6 1.6 gather_fusion.2
  12.2 1.6 gather_fusion.3
  13.8 1.5 copy.54
  15.3 37.0 %all-gather.5.cloned.1.call-done = bf16[1,128,4096]{2,1,0:T(8,128)(2,1)} async-done(((bf16[1,16,4096]{2,1,0:T(8,128)(2,1)}), bf16[1,128,4096]{2,1,0:T(8,128)(2,1)}) %all-gather.5.cloned.1.call-update) | async-done | bytes 1048592 | tf_op jit(solution)/shard_map/all_gather | solution.py:46
  52.4 1.6 copy.52
  55.7 1.0 fusion.21
  56.8 1.9 fusion.17
  61.5 1.8 fusion.27
  63.4 1.9 fusion.13
  65.2 1.8 fusion.25
  67.1 19.5 %pmax.7 = bf16[128,32]{0,1:T(8,128)(2,1)S(1)} all-reduce(bf16[128,32]{0,1:T(8,128)(2,1)S(1)} %fusion.81), channel_id=1, replica_groups=mesh['seq'=8,'grp'=4] {'seq'}, use_global_device_ids=true, to_apply=%region_4.0 | all-reduce | flops 4096 | bytes 16384 | tf_op jit(solution)/shard_map/pmax | solution.py:82
  86.6 2.5 fusion.29
  89.2 1.2 gather_fusion.4
  90.5 1.2 gather_fusion.5
  91.8 1.2 gather_fusion.6
  94.3 30.6 %all-gather.1 = bf16[1,128,512]{2,1,0:T(8,128)(2,1)S(1)} all-gather(bf16[1,16,512]{2,1,0:T(8,128)(2,1)S(1)} %copy-done.8), channel_id=3, replica_groups=mesh['seq'=8,'grp'=4] {'seq'}, dimensions={1}, use_global_device_ids=true | all-gather | bytes 147456 | tf_op jit(solution)/shard_map/all_gather | solution.py:97
  124.9 30.6 %all-gather.2 = bf16[1,128,512]{2,1,0:T(8,128)(2,1)S(1)} all-gather(bf16[1,16,512]{2,1,0:T(8,128)(2,1)S(1)} %copy-done.9), channel_id=4, replica_groups=mesh['seq'=8,'grp'=4] {'seq'}, dimensions={1}, use_global_device_ids=true | all-gather | bytes 147456 | tf_op jit(solution)/shard_map/all_gather | solution.py:98
  155.6 17.7 %all-reduce = bf16[128,32]{0,1:T(8,128)(2,1)S(1)} all-reduce(bf16[128,32]{0,1:T(8,128)(2,1)S(1)} %get-tuple-element.7), channel_id=6, replica_groups=mesh['seq'=8,'grp'=4] {'seq'}, use_global_device_ids=true, to_apply=%region_11.12.clone | all-reduce | flops 4096 | bytes 16384
  173.7 1.1 fusion.53
  174.8 3.9 %convolution_convert_fusion.1 = bf16[128,4096]{1,0:T(8,128)(2,1)} fusion(bf16[128,512]{0,1:T(8,128)(2,1)S(1)} %bitcast.167, bf16[512,4096]{1,0:T(8,128)(2,1)} %param.20), kind=kOutput, calls=%fused_computation.18 | convolution fusion | flops 537395200 | bytes 5373952 | tf_op jit(solution)/shard_map/dot_general | solution.py:131
  179.8 61.7 %reduce-scatter.5.cloned.1.call-done = bf16[16,4096]{1,0:T(8,128)(2,1)} async-done(((bf16[128,4096]{1,0:T(8,128)(2,1)}), bf16[16,4096]{1,0:T(8,128)(2,1)}) %reduce-scatter.5.cloned.1.call-update) | async-done | bytes 131088 | tf_op jit(solution)/shard_map/reduce_scatter | solution.py:130
  241.5 1.1 multiply_reduce_fusion.4
  242.5 1.7 fusion.12
  244.2 52.2 %all_to_all.10 = bf16[32,8,4096]{2,1,0:T(8,128)(2,1)S(1)} all-to-all(bf16[32,8,4096]{2,1,0:T(8,128)(2,1)S(1)} %fusion.12), channel_id=1, replica_groups=mesh['seq'=8,'grp'=4] {'seq','grp'}, dimensions={0} | all-to-all | bytes 4194304 | tf_op jit(solution)/shard_map/all_to_all | solution.py:168
  296.3 4.6 %fusion.4 = f32[256,768]{1,0:T(8,128)S(1)} fusion(bf16[1,4096,768]{2,1,0:T(8,128)(2,1)} %param.25, bf16[32,8,4096]{2,1,0:T(8,128)(2,1)S(1)} %all_to_all.10), kind=kOutput, calls=%fused_computation.12 | convolution fusion | flops 1610612736 | bytes 9175040 | tf_op jit(solution)/shard_map/dot_general | solution.py:170
  300.9 10.5 %fusion.9 = bf16[32,8,4096]{2,1,0:T(8,128)(2,1)} fusion(bf16[1,768,4096]{2,1,0:T(8,128)(2,1)} %param.27, bf16[1,4096,768]{2,1,0:T(8,128)(2,1)} %param.26, bf16[32,8,4096]{2,1,0:T(8,128)(2,1)S(1)} %all_to_all.10, f32[256,768]{1,0:T(8,128)S(1)} %fusion.4), kind=kOutput, calls=%fused_computation.16 | convolution fusion | flops 3223453696 | bytes 17563648 | tf_op jit(solution)/shard_map/dot_general | solution.py:174
  311.5 3.7 all-to-all-start.1
  316.0 47.9 %all-to-all-done.1 = bf16[32,8,4096]{2,1,0:T(8,128)(2,1)S(1)} async-done(((bf16[32,8,4096]{2,1,0:T(8,128)(2,1)}), bf16[32,8,4096]{2,1,0:T(8,128)(2,1)S(1)}, u32[]{:S(2)}, u32[]{:S(2)}) %all-to-all-start.1) | async-done | bytes 2097184 | tf_op jit(solution)/shard_map/all_to_all | solution.py:173
  363.9 1.2 gather_fusion.7
  365.9 1.6 fusion.66
  (82 shorter events, 9.1 us)
Async XLA Ops:
  6.5 308.9 %copy-start = (bf16[4096,32]{0,1:T(8,128)(2,1)S(1)}, bf16[4096,32]{0,1:T(8,128)(2,1)}, u32[]{:S(2)}) copy-start(bf16[4096,32]{0,1:T(8,128)(2,1)} %param.23) | copy-start | bytes 786436
  6.5 45.8 %all-gather.5.cloned.1.call-start = ((), (), s32[]{:S(2)}) async-start(), calls=%async_computation.6 | async-start | bytes 1179648 | tf_op jit(solution)/shard_map/all_gather | solution.py:46
  7.3 166.4 %reduce-scatter.3.cloned.1.call-start = ((), (), s32[]{:S(2)}) async-start(), calls=%async_computation.4 | async-start | bytes 1179648 | tf_op jit(solution)/shard_map/reduce_scatter | solution.py:91
  7.3 46.7 %copy-start.4 = (bf16[1,1024,512]{2,1,0:T(8,128)(2,1)S(1)}, bf16[1,1024,512]{2,1,0:T(8,128)(2,1)}, u32[]{:S(2)}) copy-start(bf16[1,1024,512]{2,1,0:T(8,128)(2,1)} %param.15) | copy-start | bytes 3145732
  58.6 1.2 copy-start.5
  65.2 24.0 %copy-start.1 = (s32[1,128]{1,0:T(1,128)S(1)}, s32[1,128]{1,0:T(1,128)}, u32[]{:S(2)}) copy-start(s32[1,128]{1,0:T(1,128)} %param.19) | copy-start | bytes 1540
  67.1 25.9 %copy-start.10 = (u32[32]{0:T(128)S(1)}, u32[32]{0:T(128)}, u32[]{:S(2)}) copy-start(u32[32]{0:T(128)} %constant.79) | copy-start | bytes 388
  67.1 27.2 %copy-start.8 = (bf16[1,16,512]{2,1,0:T(8,128)(2,1)S(1)}, bf16[1,16,512]{2,1,0:T(8,128)(2,1)}, u32[]{:S(2)}) copy-start(bf16[1,16,512]{2,1,0:T(8,128)(2,1)} %param.17) | copy-start | bytes 49156
  67.1 57.8 %copy-start.9 = (bf16[1,16,512]{2,1,0:T(8,128)(2,1)S(1)}, bf16[1,16,512]{2,1,0:T(8,128)(2,1)}, u32[]{:S(2)}) copy-start(bf16[1,16,512]{2,1,0:T(8,128)(2,1)} %param.18) | copy-start | bytes 49156
  89.1 152.3 %reduce-scatter.5.cloned.1.call-start = ((), (), s32[]{:S(2)}) async-start(), calls=%async_computation.5 | async-start | bytes 1179648 | tf_op jit(solution)/shard_map/reduce_scatter | solution.py:130
  173.3 5.5 %copy-start.7 = (s32[1,16,8]{1,2,0:T(8,128)S(1)}, s32[1,16,8]{1,2,0:T(8,128)}, u32[]{:S(2)}) copy-start(s32[1,16,8]{1,2,0:T(8,128)} %param.24) | copy-start | bytes 1540
  173.5 67.9 %copy-start.2 = (bf16[1,16,4096]{2,1,0:T(8,128)(2,1)S(1)}, bf16[1,16,4096]{2,1,0:T(8,128)(2,1)}, u32[]{:S(2)}) copy-start(bf16[1,16,4096]{2,1,0:T(8,128)(2,1)} %param.21) | copy-start | bytes 393220
  173.5 69.0 %copy-start.6 = (f32[4096]{0:T(1024)S(1)}, f32[4096]{0:T(1024)}, u32[]{:S(2)}) copy-start(f32[4096]{0:T(1024)} %param.22) | copy-start | bytes 49156
  311.5 4.0 %copy-start.3 = (bf16[16,4096]{1,0:T(8,128)(2,1)S(1)}, bf16[16,4096]{1,0:T(8,128)(2,1)}, u32[]{:S(2)}) copy-start(bf16[16,4096]{1,0:T(8,128)(2,1)} %reduce-scatter.5.cloned.1.call-done) | copy-start | bytes 393220
  311.5 52.4 %all-to-all-start.1 = ((bf16[32,8,4096]{2,1,0:T(8,128)(2,1)}), bf16[32,8,4096]{2,1,0:T(8,128)(2,1)S(1)}, u32[]{:S(2)}, u32[]{:S(2)}) async-start(bf16[32,8,4096]{2,1,0:T(8,128)(2,1)} %fusion.9), calls=%async_computation.3 | async-start | bytes 4194304 | tf_op jit(solution)/shard_map/all_to_all | solution.py:173
Sparse Core Ops, SparseCore 0:
  9.5 42.8 all-gather.4
  89.2 61.0 reduce-scatter.2
  178.9 62.5 reduce-scatter.4
where the time goes:
time: 375 us; the launch traced here: 374 us
  blocking collectives  151 us (40%)
  waiting for transfers between devices  147 us (39%)
  matrix products  31.3 us (8%)
  local copies, waits for them, and re-layouts  15.9 us (4%)
  between operations  14.3 us (4%)
  other arithmetic  10.9 us (3%)
  starting transfers between devices  3.75 us (1%)
    reduce_scatter x1, waiting for transfers between devices, local(): lax.psum_scatter(jnp.dot(attention, out_proj, preferred_element_type=jnp....  61.7 us
    all_to_all x1, blocking collectives, local(): lax.all_to_all(outgoing, ('seq', 'grp'), split_axis=0, concat_axis=0, til...  52.2 us
    all_to_all x1, waiting for transfers between devices, local(): lax.all_to_all(jnp.dot(act, down_weight, preferred_element_type=jnp.float...  47.9 us
    all_gather x1, waiting for transfers between devices, local(): all_queries = lax.all_gather(query_local, 'seq', axis=0, tiled=True)  37 us
    all_gather x1, blocking collectives, local(): lax.all_gather(suffix_keys[0], 'seq', axis=0, tiled=True)  30.6 us
    all_gather x1, blocking collectives, local(): lax.all_gather(suffix_values[0], 'seq', axis=0, tiled=True)  30.6 us
    pmax x1, blocking collectives, local(): lax.pmax(local_max.astype(jnp.bfloat16), 'seq').astype(local_max.dtype)  19.5 us
    unnamed x1, blocking collectives  17.7 us
  transfers between devices with their start and end apart: 4, of which 3 were waited for; matrix products, arithmetic and copies ran while one was open for 4% of the time, Pallas kernels for 0%

commit v1 on v0

v1 whole, which is shorter than its diff:
```python
import functools
import math

import jax
import jax.numpy as jnp
from jax import lax
from jax.experimental import pallas as pl
from jax.experimental.pallas import tpu as pltpu
from jax.sharding import PartitionSpec as P

HEADS = 32
KVH = 4
HD = 128
DEPTH = 8
EPSILON = 1e-06
MESH = pl.DeviceIdType.MESH
SCALE = HD ** (-0.5) * math.log2(math.e)
F32 = jnp.float32
BF16 = jnp.bfloat16
VLIMIT = 60 * 1024 * 1024
SEMS = 96


class Place:
    def __init__(self, n_seq, n_grp):
        self.nx = 2 ** (int(math.log2(n_seq)) // 2)
        self.nz = n_seq // self.nx
        self.ny = n_grp // 2
        s, g = lax.axis_index("seq"), lax.axis_index("grp")
        self.z, self.x = s // self.nx, lax.rem(s, self.nx)
        self.y, self.c = g // 2, lax.rem(g, 2)

    def device(self, z=None, x=None, y=None, c=None):
        z = self.z if z is None else z
        x = self.x if x is None else x
        y = self.y if y is None else y
        c = self.c if c is None else c
        return (z * self.nx + x, y * 2 + c)

    def zk(self, k):
        return lax.rem(self.z + k + self.nz, self.nz)

    def xk(self, k):
        return lax.rem(self.x + k + self.nx, self.nx)

    def yk(self, k):
        return lax.rem(self.y + k + self.ny, self.ny)


def dims(n_seq, n_grp):
    nx = 2 ** (int(math.log2(n_seq)) // 2)
    return n_seq // nx, nx, n_grp // 2


def greet(peers):
    barrier = pltpu.get_barrier_semaphore()
    for peer in peers:
        pl.semaphore_signal(barrier, inc=1, device_id=peer, device_id_type=MESH)
    pl.semaphore_wait(barrier, len(peers))


class Copies:
    def __init__(self, send_sems, recv_sems):
        self.send_sems, self.recv_sems, self.started = send_sems, recv_sems, []

    def start(self, src, dst, device):
        n = len(self.started)
        copy = pltpu.make_async_remote_copy(
            src_ref=src,
            dst_ref=dst,
            send_sem=self.send_sems.at[n],
            recv_sem=self.recv_sems.at[n],
            device_id=device,
            device_id_type=MESH,
        )
        copy.start()
        self.started.append(copy)
        return copy

    def finish(self):
        for copy in self.started:
            copy.wait_send()


def axis_peers(p, grp=True):
    peers = [p.device(z=p.zk(k)) for k in range(1, p.nz)]
    peers += [p.device(x=p.xk(k)) for k in range(1, p.nx)]
    if grp:
        peers += [p.device(y=p.yk(k)) for k in range(1, p.ny)]
        peers += [p.device(c=1 - p.c)]
    return peers


def call(kernel, outs, ins, scratch, ident):
    vmem = pl.BlockSpec(memory_space=pltpu.VMEM)
    return pl.pallas_call(
        kernel,
        out_shape=outs,
        in_specs=[vmem] * len(ins),
        out_specs=jax.tree.map(lambda _: vmem, outs),
        scratch_shapes=list(scratch)
        + [pltpu.SemaphoreType.DMA((SEMS,)), pltpu.SemaphoreType.DMA((SEMS,))],
        compiler_params=pltpu.CompilerParams(
            collective_id=ident, has_side_effects=True, vmem_limit_bytes=VLIMIT
        ),
    )(*ins)


def gather_kernel(n_seq, n_grp, in_ref, out_ref, send_sems, recv_sems):
    p = Place(n_seq, n_grp)
    greet(axis_peers(p, grp=False))
    copies = Copies(send_sems, recv_sems)
    z_copies = [
        copies.start(in_ref, out_ref.at[p.z, p.x], p.device(z=p.zk(k))) for k in range(1, p.nz)
    ]
    x_copies = [
        copies.start(in_ref, out_ref.at[p.z, p.x], p.device(x=p.xk(j))) for j in range(1, p.nx)
    ]
    out_ref[p.z, p.x] = in_ref[...]
    for k in range(1, p.nz):
        z_copies[k - 1].wait_recv()
        block = out_ref.at[p.zk(-k), p.x]
        x_copies += [copies.start(block, block, p.device(x=p.xk(j))) for j in range(1, p.nx)]
    for copy in x_copies:
        copy.wait_recv()
    copies.finish()


def prefix_kernel(group, q_ref, k_ref, v_ref, o_ref, m_ref, l_ref):
    key, value = k_ref[...], v_ref[...]
    for h in range(group):
        s = lax.dot_general(
            key, q_ref[:, h * HD : (h + 1) * HD], (((1,), (1,)), ((), ())),
            preferred_element_type=F32,
        ) * SCALE
        m = jnp.max(s, axis=0, keepdims=True)
        w = jnp.exp2(s - m)
        l_ref[h : h + 1, :] = jnp.sum(w, axis=0, keepdims=True)
        m_ref[h : h + 1, :] = m
        o_ref[h * HD : (h + 1) * HD, :] = lax.dot_general(
            value, w.astype(BF16), (((0,), (0,)), ((), ())), preferred_element_type=F32
        )


def merge_kernel(
    n_seq, n_grp, o_ref, m_ref, l_ref, out_ref, total_ref, max_ref,
    m_buf, l_buf, s_buf, x_buf, a_buf, z_buf, send_sems, recv_sems,
):
    p = Place(n_seq, n_grp)
    s, g = lax.axis_index("seq"), lax.axis_index("grp")
    own_heads = m_ref.shape[1]
    others = [lax.rem(s + j, n_seq) for j in range(1, n_seq)]
    greet([(other, g) for other in others])
    copies = Copies(send_sems, recv_sems)
    small = []
    for j, other in enumerate(others):
        small.append(copies.start(m_ref, m_buf.at[j], (other, g)))
    for j, other in enumerate(others):
        small.append(copies.start(l_ref.at[other], l_buf.at[j], (other, g)))
    for copy in small[: n_seq - 1]:
        copy.wait_recv()
    whole = m_ref[...]
    for j in range(n_seq - 1):
        whole = jnp.maximum(whole, m_buf[j])
    x_buf_copies = []
    m_buf[n_seq - 1] = whole
    order = list(range(1, p.nz)) + [0]
    for k in order:
        row = []
        for j in list(range(1, p.nx)) + [0]:
            t = p.zk(k) * p.nx + p.xk(j)
            factor = jnp.exp2(m_ref[t] - m_buf[n_seq - 1, t])
            for h in range(own_heads):
                s_buf[t, h * HD : (h + 1) * HD, :] = (
                    o_ref[t, h * HD : (h + 1) * HD, :] * factor[h : h + 1, :]
                ).astype(BF16)
            if j:
                row.append(
                    copies.start(s_buf.at[t], x_buf.at[j - 1, k], p.device(x=p.xk(j)))
                )
        x_buf_copies.append(row)
    z_copies = []
    last = None
    for k, row in zip(order, x_buf_copies):
        t = p.zk(k) * p.nx + p.x
        acc = s_buf[t].astype(F32)
        for j, copy in enumerate(row):
            copy.wait_recv()
            acc = acc + x_buf[j, k].astype(F32)
        if k:
            a_buf[k - 1] = acc.astype(BF16)
            z_copies.append(copies.start(a_buf.at[k - 1], z_buf.at[k - 1], p.device(z=p.zk(k))))
        else:
            last = acc
    out_ref[...] = last
    for copy in small[n_seq - 1 :]:
        copy.wait_recv()
    own_max = m_buf[n_seq - 1, s]
    total = l_ref[s] * jnp.exp2(m_ref[s] - own_max)
    for j in range(n_seq - 1):
        total = total + l_buf[j] * jnp.exp2(m_buf[j, s] - own_max)
    total_ref[...] = total
    max_ref[...] = own_max
    for k in range(1, p.nz):
        z_copies[k - 1].wait_recv()
        out_ref[...] += z_buf[k - 1].astype(F32)
    copies.finish()


def project_kernel(own_heads, q_ref, k_ref, v_ref, par_ref, o_ref, l_ref, m_ref, w_ref, out_ref, att_ref):
    rows = q_ref.shape[0]

    @pl.when(pl.program_id(0) == 0)
    def _():
        j_index = lax.broadcasted_iota(jnp.int32, (rows, rows), 0)
        i_index = lax.broadcasted_iota(jnp.int32, (rows, rows), 1)
        step = (par_ref[...] == j_index).astype(F32) + (i_index == j_index).astype(F32)
        paths, power = step, step
        for _ in range(int(math.log2(DEPTH)) - 1):
            power = jnp.dot(power.astype(BF16), power.astype(BF16), preferred_element_type=F32)
            paths = jnp.dot(paths.astype(BF16), power.astype(BF16), preferred_element_type=F32)
        seen = paths > 0.5
        for h in range(own_heads):
            s = lax.dot_general(
                k_ref[...], q_ref[:, h * HD : (h + 1) * HD], (((1,), (1,)), ((), ())),
                preferred_element_type=F32,
            ) * SCALE
            s = jnp.where(seen, s, -jnp.inf)
            before = m_ref[h : h + 1, :]
            top = jnp.maximum(before, jnp.max(s, axis=0, keepdims=True))
            w = jnp.exp2(s - top)
            scale = jnp.exp2(before - top)
            total = l_ref[h : h + 1, :] * scale + jnp.sum(w, axis=0, keepdims=True)
            o = lax.dot_general(
                v_ref[...], w.astype(BF16), (((0,), (0,)), ((), ())), preferred_element_type=F32
            )
            o = (o_ref[h * HD : (h + 1) * HD, :] * scale + o) / total
            att_ref[:, h * HD : (h + 1) * HD] = o.T.astype(BF16)

    out_ref[...] = jnp.dot(att_ref[...], w_ref[...], preferred_element_type=F32).astype(BF16)


def norm_kernel(
    n_seq, n_grp, experts, proj_ref, res_ref, gain_ref, router_ref, chosen_ref,
    mixed_ref, out_ref, x_buf, a_buf, z_buf, send_sems, recv_sems,
):
    p = Place(n_seq, n_grp)
    greet(axis_peers(p))
    copies = Copies(send_sems, recv_sems)
    order = list(range(1, p.nz)) + [0]
    x_copies = [
        [
            copies.start(proj_ref.at[p.zk(k), p.xk(j)], x_buf.at[j - 1, k], p.device(x=p.xk(j)))
            for j in range(1, p.nx)
        ]
        for k in order
    ]
    z_copies = []
    mixed = None
    for k, row in zip(order, x_copies):
        acc = proj_ref[p.zk(k), p.x].astype(F32)
        for j, copy in enumerate(row):
            copy.wait_recv()
            acc = acc + x_buf[j, k].astype(F32)
        if k:
            a_buf[k - 1] = acc.astype(BF16)
            z_copies.append(copies.start(a_buf.at[k - 1], z_buf.at[k - 1], p.device(z=p.zk(k))))
        else:
            mixed_ref[...] = acc + res_ref[...].astype(F32)
    for k in range(1, p.nz):
        z_copies[k - 1].wait_recv()
        mixed_ref[...] += z_buf[k - 1].astype(F32)
    mixed = mixed_ref[...]
    inverse = lax.rsqrt(jnp.mean(mixed * mixed, axis=1, keepdims=True) + EPSILON)
    normed = (mixed * inverse * gain_ref[...]).astype(BF16)
    width = normed.shape[1]
    own = out_ref.at[p.c, p.z, p.x, p.y]
    own[:, :width] = normed
    logits = jnp.dot(normed, router_ref[...], preferred_element_type=F32)
    sig = jax.nn.sigmoid(logits) * chosen_ref[...]
    lane = lax.broadcasted_iota(jnp.int32, sig.shape, 1)
    gates = sig / jnp.sum(jnp.where(lane < experts, sig, 0.0), axis=1, keepdims=True)
    high = gates.astype(BF16).astype(F32)
    own[:, width:] = jnp.where(lane < experts, high, gates - high).astype(BF16)

    half = width // 2
    cuts = (pl.ds(0, half), pl.ds(half, out_ref.shape[5] - half))
    a, b = cuts
    c = p.c
    z_copies = []
    for k in range(1, p.nz):
        z_copies.append(
            [
                copies.start(
                    out_ref.at[c, p.z, p.x, p.y, :, cut], out_ref.at[c, p.z, p.x, p.y, :, cut],
                    p.device(z=p.zk(k)),
                )
                for cut in cuts
            ]
        )
    first, second, core = [], [], []
    ks = list(range(p.nz))

    def spread(k):
        block = (c, p.zk(-k), p.x, p.y, slice(None))
        row = []
        for j in range(1, p.nx):
            ref = out_ref.at[block + (a,)]
            row.append(copies.start(ref, ref, p.device(x=p.xk(j))))
        for j in range(1, p.ny):
            ref = out_ref.at[block + (b,)]
            row.append(copies.start(ref, ref, p.device(y=p.yk(j))))
        return row

    def widen(k, row):
        for copy in row:
            copy.wait_recv()
        done = []
        for j in range(1, p.ny):
            ref = out_ref.at[c, p.zk(-k), :, p.y, :, a]
            done.append(copies.start(ref, ref, p.device(y=p.yk(j))))
        for j in range(1, p.nx):
            ref = out_ref.at[c, p.zk(-k), p.x, :, :, b]
            done.append(copies.start(ref, ref, p.device(x=p.xk(j))))
        return done

    def share(k, row):
        for copy in row:
            copy.wait_recv()
        ref = out_ref.at[c, p.zk(-k)]
        return copies.start(ref, ref, p.device(c=1 - c))

    for k in ks:
        if k:
            for copy in z_copies[k - 1]:
                copy.wait_recv()
        first.append(spread(k))
        if k >= 1:
            second.append(widen(k - 1, first[k - 1]))
        if k >= 2:
            core.append(share(k - 2, second[k - 2]))
    second.append(widen(ks[-1], first[-1]))
    core.append(share(ks[-2], second[-2]))
    core.append(share(ks[-1], second[-1]))
    for copy in core:
        copy.wait_recv()
    copies.finish()


def combine_kernel(
    n_seq, n_grp, in_ref, mixed_ref, out_ref,
    c_buf, acc, a1, b1, a2, b2, a3, b3, a4, b4, a5, b5, send_sems, recv_sems,
):
    p = Place(n_seq, n_grp)
    greet(axis_peers(p))
    copies = Copies(send_sems, recv_sems)
    width = out_ref.shape[1]
    half = width // 2
    a, b = pl.ds(0, half), pl.ds(half, width - half)
    order = list(range(1, p.nz)) + [0]
    core = [
        copies.start(in_ref.at[1 - p.c, p.zk(k)], c_buf.at[k], p.device(c=1 - p.c)) for k in order
    ]
    first, second, third = [], [], []

    def core_sum(i):
        k = order[i]
        core[i].wait_recv()
        for x in range(p.nx):
            for y in range(p.ny):
                acc[k, x, y] = (
                    in_ref[p.c, p.zk(k), x, y].astype(F32) + c_buf[k, x, y].astype(F32)
                ).astype(BF16)
        row = []
        for j in range(1, p.ny):
            row.append(
                copies.start(acc.at[k, :, p.yk(j), :, a], a1.at[j - 1, k], p.device(y=p.yk(j)))
            )
        for j in range(1, p.nx):
            row.append(
                copies.start(acc.at[k, p.xk(j), :, :, b], b1.at[j - 1, k], p.device(x=p.xk(j)))
            )
        first.append(row)

    def first_sum(i):
        k = order[i]
        for copy in first[i]:
            copy.wait_recv()
        for x in range(p.nx):
            total = acc[k, x, p.y, :, a].astype(F32)
            for j in range(p.ny - 1):
                total = total + a1[j, k, x].astype(F32)
            a2[k, x] = total.astype(BF16)
        for y in range(p.ny):
            total = acc[k, p.x, y, :, b].astype(F32)
            for j in range(p.nx - 1):
                total = total + b1[j, k, y].astype(F32)
            b2[k, y] = total.astype(BF16)
        row = []
        for j in range(1, p.nx):
            row.append(copies.start(a2.at[k, p.xk(j)], a3.at[j - 1, k], p.device(x=p.xk(j))))
        for j in range(1, p.ny):
            row.append(copies.start(b2.at[k, p.yk(j)], b3.at[j - 1, k], p.device(y=p.yk(j))))
        second.append(row)

    def second_sum(i):
        k = order[i]
        for copy in second[i]:
            copy.wait_recv()
        left = a2[k, p.x].astype(F32)
        for j in range(p.nx - 1):
            left = left + a3[j, k].astype(F32)
        right = b2[k, p.y].astype(F32)
        for j in range(p.ny - 1):
            right = right + b3[j, k].astype(F32)
        if k:
            a4[k - 1] = left.astype(BF16)
            b4[k - 1] = right.astype(BF16)
            third.append(copies.start(a4.at[k - 1], a5.at[k - 1], p.device(z=p.zk(k))))
            third.append(copies.start(b4.at[k - 1], b5.at[k - 1], p.device(z=p.zk(k))))
            return None
        return left, right

    n = len(order)
    for i in range(n):
        core_sum(i)
        if i >= 1:
            first_sum(i - 1)
        if i >= 2:
            second_sum(i - 2)
    first_sum(n - 1)
    second_sum(n - 2)
    left, right = second_sum(n - 1)
    left = left + mixed_ref[:, a]
    right = right + mixed_ref[:, b]
    for copy in third:
        copy.wait_recv()
    for k in range(p.nz - 1):
        left = left + a5[k].astype(F32)
        right = right + b5[k].astype(F32)
    out_ref[:, a] = left.astype(BF16)
    out_ref[:, b] = right.astype(BF16)
    copies.finish()


def local(
    queries, prefix_keys, prefix_values, suffix_keys, suffix_values, parents, out_proj,
    residual, norm_gain, router, routes, expert_gate, expert_up, expert_down,
):
    n_seq, n_grp = lax.axis_size("seq"), lax.axis_size("grp")
    nz, nx, ny = dims(n_seq, n_grp)
    s, g = lax.axis_index("seq"), lax.axis_index("grp")
    rows, width = queries.shape[1], queries.shape[2]
    total_rows = rows * n_seq
    keys = prefix_keys.shape[1]
    kv_width = suffix_keys.shape[2]
    group = HEADS // KVH
    own_heads = HEADS // n_seq
    own_width = own_heads * HD
    vmem = pltpu.VMEM

    packed = jnp.concatenate([queries[0], suffix_keys[0], suffix_values[0]], axis=1)
    pack_width = packed.shape[1]
    gathered = call(
        functools.partial(gather_kernel, n_seq, n_grp),
        jax.ShapeDtypeStruct((nz, nx, rows, pack_width), BF16),
        [packed], [], 0,
    ).reshape(total_rows, pack_width)

    o, m, l = pl.pallas_call(
        functools.partial(prefix_kernel, group),
        grid=(KVH,),
        in_specs=[
            pl.BlockSpec((total_rows, group * HD), lambda i: (0, i)),
            pl.BlockSpec((keys, HD), lambda i: (0, i)),
            pl.BlockSpec((keys, HD), lambda i: (0, i)),
        ],
        out_specs=[
            pl.BlockSpec((group * HD, total_rows), lambda i: (i, 0)),
            pl.BlockSpec((group, total_rows), lambda i: (i, 0)),
            pl.BlockSpec((group, total_rows), lambda i: (i, 0)),
        ],
        out_shape=[
            jax.ShapeDtypeStruct((HEADS * HD, total_rows), F32),
            jax.ShapeDtypeStruct((HEADS, total_rows), F32),
            jax.ShapeDtypeStruct((HEADS, total_rows), F32),
        ],
        compiler_params=pltpu.CompilerParams(vmem_limit_bytes=VLIMIT),
    )(gathered, prefix_keys[0], prefix_values[0])

    o_own, l_own, m_own = call(
        functools.partial(merge_kernel, n_seq, n_grp),
        [
            jax.ShapeDtypeStruct((own_width, total_rows), F32),
            jax.ShapeDtypeStruct((own_heads, total_rows), F32),
            jax.ShapeDtypeStruct((own_heads, total_rows), F32),
        ],
        [
            o.reshape(n_seq, own_width, total_rows),
            m.reshape(n_seq, own_heads, total_rows),
            l.reshape(n_seq, own_heads, total_rows),
        ],
        [
            vmem((n_seq, n_seq, own_heads, total_rows), F32),
            vmem((n_seq - 1, own_heads, total_rows), F32),
            vmem((n_seq, own_width, total_rows), BF16),
            vmem((nx - 1, nz, own_width, total_rows), BF16),
            vmem((nz - 1, own_width, total_rows), BF16),
            vmem((nz - 1, own_width, total_rows), BF16),
        ],
        1,
    )

    kv_index = s * own_heads // group
    own_q = lax.dynamic_slice_in_dim(gathered, s * own_width, own_width, 1)
    own_k = lax.dynamic_slice_in_dim(gathered, width + kv_index * HD, HD, 1)
    own_v = lax.dynamic_slice_in_dim(gathered, width + kv_width + kv_index * HD, HD, 1)
    tile = min(1024, width)
    whole = lambda *shape: pl.BlockSpec(shape, lambda i: (0,) * len(shape))
    projected = pl.pallas_call(
        functools.partial(project_kernel, own_heads),
        grid=(width // tile,),
        in_specs=[
            whole(total_rows, own_width), whole(total_rows, HD), whole(total_rows, HD),
            whole(1, total_rows), whole(own_width, total_rows), whole(own_heads, total_rows),
            whole(own_heads, total_rows), pl.BlockSpec((own_width, tile), lambda i: (0, i)),
        ],
        out_specs=pl.BlockSpec((total_rows, tile), lambda i: (0, i)),
        out_shape=jax.ShapeDtypeStruct((total_rows, width), BF16),
        scratch_shapes=[vmem((total_rows, own_width), BF16)],
        compiler_params=pltpu.CompilerParams(vmem_limit_bytes=VLIMIT),
    )(own_q, own_k, own_v, parents, o_own, l_own, m_own, out_proj)

    experts = router.shape[1]
    lanes = -(-2 * experts // 128) * 128
    chosen = jnp.sum(
        (routes[0][:, :, None] == jnp.arange(experts, dtype=jnp.int32)).astype(F32), axis=1
    )
    pad = ((0, 0), (0, lanes - 2 * experts))
    chosen = jnp.pad(jnp.concatenate([chosen, chosen], axis=1), pad)
    router_wide = jnp.pad(jnp.concatenate([router, router], axis=1), pad)
    mixed, arrived = call(
        functools.partial(norm_kernel, n_seq, n_grp, experts),
        [
            jax.ShapeDtypeStruct((rows, width), F32),
            jax.ShapeDtypeStruct((2, nz, nx, ny, rows, width + lanes), BF16),
        ],
        [
            projected.reshape(nz, nx, rows, width), residual[0], norm_gain[None], router_wide,
            chosen,
        ],
        [
            vmem((nx - 1, nz, rows, width), BF16),
            vmem((nz - 1, rows, width), BF16),
            vmem((nz - 1, rows, width), BF16),
        ],
        2,
    )

    flat = arrived.reshape(-1, width + lanes)
    x = flat[:, :width]
    parts = flat[:, width:].astype(F32)
    expert = s * n_grp + g
    lane = jnp.arange(lanes, dtype=jnp.int32)
    mine = (lane == expert) | (lane == expert + experts)
    gate = jnp.sum(jnp.where(mine[None, :], parts, 0.0), axis=1, keepdims=True)
    gate_part = jnp.dot(x, expert_gate[0], preferred_element_type=F32)
    up_part = jnp.dot(x, expert_up[0], preferred_element_type=F32)
    act = (jax.nn.silu(gate_part) * up_part).astype(BF16)
    result = jnp.dot(act, expert_down[0], preferred_element_type=F32).astype(BF16)
    weighted = (result.astype(F32) * gate).astype(BF16)

    half = width // 2
    out = call(
        functools.partial(combine_kernel, n_seq, n_grp),
        jax.ShapeDtypeStruct((rows, width), BF16),
        [weighted.reshape(2, nz, nx, ny, rows, width), mixed],
        [
            vmem((nz, nx, ny, rows, width), BF16),
            vmem((nz, nx, ny, rows, width), BF16),
            vmem((ny - 1, nz, nx, rows, half), BF16),
            vmem((nx - 1, nz, ny, rows, half), BF16),
            vmem((nz, nx, rows, half), BF16),
            vmem((nz, ny, rows, half), BF16),
            vmem((nx - 1, nz, rows, half), BF16),
            vmem((ny - 1, nz, rows, half), BF16),
            vmem((nz - 1, rows, half), BF16),
            vmem((nz - 1, rows, half), BF16),
            vmem((nz - 1, rows, half), BF16),
            vmem((nz - 1, rows, half), BF16),
        ],
        3,
    )
    return out[None]


def solution(mesh):
    in_specs = (
        P("grp", "seq", None),
        P("grp", "seq", None),
        P("grp", "seq", None),
        P("grp", "seq", None),
        P("grp", "seq", None),
        P("grp", None),
        P("seq", None),
        P("grp", "seq", None),
        P(),
        P(),
        P("grp", "seq", None),
        P(("seq", "grp"), None, None),
        P(("seq", "grp"), None, None),
        P(("seq", "grp"), None, None),
    )
    out_specs = P("grp", "seq", None)
    return jax.shard_map(local, mesh=mesh, in_specs=in_specs, out_specs=out_specs, check_vma=False)
```

time: 375 us -> 192 us (0.51)
  Pallas kernels: 0 us -> 155 us
  blocking collectives: 151 us -> 0 us
  waiting for transfers between devices: 147 us -> 0 us
  between operations: 14.3 us -> 0.06 us
  local copies, waits for them, and re-layouts: 15.9 us -> 6.75 us
  matrix products: 31.3 us -> 23.9 us
  other arithmetic: 10.9 us -> 5.09 us
  starting transfers between devices: 3.75 us -> 0 us
    pallas_call x0 -> x6, Pallas kernels: none -> 155 us  [the longest x4 139 us: call(): pl.pallas_call(kernel, out_shape=outs, in_specs=[vmem] * len(ins), out_sp...]
    reduce_scatter x2 -> x0, waiting for transfers between devices: 61.7 us -> none  [the longest x1 61.7 us: local(): lax.psum_scatter(jnp.dot(attention, out_proj, preferred_element_type=jnp....]
    all_gather x2 -> x0, blocking collectives: 61.3 us -> none  [the longest x1 30.6 us: local(): lax.all_gather(suffix_keys[0], 'seq', axis=0, tiled=True)]
    all_to_all x1 -> x0, blocking collectives: 52.2 us -> none  [local(): lax.all_to_all(outgoing, ('seq', 'grp'), split_axis=0, concat_axis=0, til...]
    all_to_all x1 -> x0, waiting for transfers between devices: 47.9 us -> none  [local(): lax.all_to_all(jnp.dot(act, down_weight, preferred_element_type=jnp.float...]
    all_gather x1 -> x0, waiting for transfers between devices: 37 us -> none  [local(): all_queries = lax.all_gather(query_local, 'seq', axis=0, tiled=True)]
    pmax x1 -> x0, blocking collectives: 19.5 us -> none  [local(): lax.pmax(local_max.astype(jnp.bfloat16), 'seq').astype(local_max.dtype)]
    unnamed x1 -> x0, blocking collectives: 17.7 us -> none
  transfers between devices with their start and end apart: 4 -> 0, of which waited for: 3 -> 0; matrix products, arithmetic and copies ran while one was open for 4% -> 0% of each run, Pallas kernels for 0% -> 0%
where the time goes in v1:
time: 192 us; the launch traced here: 191 us
  Pallas kernels  155 us (81%)
  matrix products  23.9 us (12%)
  local copies, waits for them, and re-layouts  6.75 us (4%)
  other arithmetic  5.09 us (3%)
    pallas_call x4, Pallas kernels, call(): pl.pallas_call(kernel, out_shape=outs, in_specs=[vmem] * len(ins), out_sp...  139 us
    dot_general x1, matrix products, local(): jnp.dot(act, expert_down[0], preferred_element_type=F32).astype(BF16)  16.6 us
    pallas_call x1, Pallas kernels, local(): pl.pallas_call(functools.partial(prefix_kernel, group), grid=(KVH,), in_s...  10.2 us
    dot_general x1, matrix products, local(): gate_part = jnp.dot(x, expert_gate[0], preferred_element_type=F32)  7.23 us
    pallas_call x1, Pallas kernels, local(): pl.pallas_call(functools.partial(project_kernel, own_heads), grid=(width...  6.06 us

profile of v1, /device:TPU:0, one launch (start us, length us, event | category | flops | bytes accessed | tf_op | source)
XLA Modules:
  0.0 191.0 jit_solution(15649236104930606436)
XLA Ops:
  0.0 0.8 copy.20
  0.8 0.1 convert_reduce_fusion
  0.9 0.7 select_maximum_fusion.chosen_ref
  1.5 1.6 pad_maximum_fusion.in_ref
  3.2 1.5 copy.18
  4.6 1.7 fusion.23.router_ref
  6.3 29.6 %shard_map.136 = bf16[4,2,16,5120]{3,2,1,0:T(8,128)(2,1)} custom-call(bf16[16,5120]{1,0:T(8,128)(2,1)} %pad_maximum_fusion.in_ref), custom_call_target="tpu_custom_call" | custom-call | tf_op jit(solution)/shard_map/pallas_call | solution.py:96
  36.0 1.4 constant_dynamic-slice_fusion
  37.4 1.6 constant_dynamic-slice_fusion.2.q_ref
  38.9 10.2 %shard_map.137 = (f32[4096,128]{1,0:T(8,128)}, f32[32,128]{1,0:T(8,128)}, f32[32,128]{1,0:T(8,128)}) custom-call(bf16[128,5120]{1,0:T(8,128)(2,1)} %bitcast.35, bf16[1024,512]{1,0:T(8,128)(2,1)} %bitcast.39, bf16[1024,512]{1,0:T(8,128)(2,1)} %bitcast.40), custom_call_target="tpu_custom_call" | custom-call | tf_op jit(solution)/shard_map/pallas_call | solution.py:470
  49.1 27.2 %shard_map.138 = (f32[512,128]{1,0:T(8,128)}, f32[4,128]{1,0:T(4,128)}, f32[4,128]{1,0:T(4,128)}) custom-call(f32[8,512,128]{2,1,0:T(8,128)} %bitcast.38, f32[8,4,128]{2,1,0:T(4,128)} %bitcast.45, f32[8,4,128]{2,1,0:T(4,128)} %bitcast.46), custom_call_target="tpu_custom_call" | custom-call | tf_op jit(solution)/shard_map/pallas_call | solution.py:96
  76.3 6.1 %shard_map.139 = bf16[128,4096]{1,0:T(8,128)(2,1)} custom-call(bf16[128,512]{1,0:T(8,128)(2,1)} %constant_dynamic-slice_fusion.2.q_ref, bf16[128,128]{1,0:T(8,128)(2,1)} %get-tuple-element.22.k_ref, bf16[128,128]{1,0:T(8,128)(2,1)} %get-tuple-element.21.v_ref, s32[1,128]{1,0:T(1,128)} %par_ref.1, f32[512,128]{1,0:T(8,128)} %get-tuple-element.16.o_ref, ...), custom_call_target="tpu_custom_call" | custom-call | tf_op jit(solution)/shard_map/pallas_call | solution.py:520
  82.4 47.0 %shard_map.140 = (f32[16,4096]{1,0:T(8,128)}, bf16[2,4,2,2,16,4224]{5,4,3,2,1,0:T(8,128)(2,1)}) custom-call(bf16[4,2,16,4096]{3,2,1,0:T(8,128)(2,1)} %bitcast.36, bf16[16,4096]{1,0:T(8,128)(2,1)} %bitcast.42, f32[1,4096]{1,0:T(1,128)} %bitcast.44, bf16[4096,128]{1,0:T(8,128)(2,1)} %fusion.23.router_ref, f32[16,128]{1,0:T(8,128)} %select_maximum_fusion.chosen_ref), custom_call_target="tpu_custom_call" | custom-call | tf_op jit(solution)/shard_map/pallas_call | solution.py:96
  129.4 1.0 select_reduce_fusion
  130.4 7.2 %fusion.4 = f32[512,768]{1,0:T(8,128)S(1)} fusion(bf16[1,4096,768]{2,1,0:T(8,128)(2,1)} %param.25, bf16[512,4224]{1,0:T(8,128)(2,1)} %bitcast.51), kind=kOutput, calls=%fused_computation.5 | convolution fusion | flops 3221225472 | bytes 12058624 | tf_op jit(solution)/shard_map/dot_general | solution.py:567
  137.6 16.6 %multiply_convert_fusion = bf16[512,4096]{1,0:T(8,128)(2,1)} fusion(bf16[1,768,4096]{2,1,0:T(8,128)(2,1)} %param.27, f32[512]{0:T(512)S(1)} %select_reduce_fusion, f32[512,768]{1,0:T(8,128)S(1)} %fusion.4, bf16[1,4096,768]{2,1,0:T(8,128)(2,1)} %param.26, bf16[512,4224]{1,0:T(8,128)(2,1)} %bitcast.52), kind=kOutput, calls=%fused_computation | convolution fusion | flops 6453198848 | bytes 22546432 | tf_op jit(solution)/shard_map/dot_general | solution.py:570
  154.3 35.2 %shard_map.141 = bf16[16,4096]{1,0:T(8,128)(2,1)} custom-call(bf16[2,4,2,2,16,4096]{5,4,3,2,1,0:T(8,128)(2,1)} %bitcast.37, f32[16,4096]{1,0:T(8,128)} %get-tuple-element.20.mixed_ref), custom_call_target="tpu_custom_call" | custom-call | tf_op jit(solution)/shard_map/pallas_call | solution.py:96
  189.5 1.6 copy.22
  (1 shorter events, 0.0 us)

commit v2 on v1

--- a/solution.py
+++ b/solution.py
@@ -443,6 +443,27 @@
     copies.finish()
 
 
+def expert_kernel(x_ref, gate_w_ref, up_w_ref, down_w_ref, gate_ref, out_ref, acc_ref):
+    i, last = pl.program_id(1), pl.num_programs(1) - 1
+    x = x_ref[:, : out_ref.shape[1]]
+    gate_part = jnp.dot(x, gate_w_ref[...], preferred_element_type=F32)
+    up_part = jnp.dot(x, up_w_ref[...], preferred_element_type=F32)
+    act = (jax.nn.silu(gate_part) * up_part).astype(BF16)
+    part = jnp.dot(act, down_w_ref[...], preferred_element_type=F32)
+
+    @pl.when(i == 0)
+    def _():
+        acc_ref[...] = part
+
+    @pl.when(i > 0)
+    def _():
+        acc_ref[...] += part
+
+    @pl.when(i == last)
+    def _():
+        out_ref[...] = (acc_ref[...].astype(BF16).astype(F32) * gate_ref[...]).astype(BF16)
+
+
 def local(
     queries, prefix_keys, prefix_values, suffix_keys, suffix_values, parents, out_proj,
     residual, norm_gain, router, routes, expert_gate, expert_up, expert_down,
@@ -558,17 +579,28 @@
     )
 
     flat = arrived.reshape(-1, width + lanes)
-    x = flat[:, :width]
     parts = flat[:, width:].astype(F32)
     expert = s * n_grp + g
     lane = jnp.arange(lanes, dtype=jnp.int32)
     mine = (lane == expert) | (lane == expert + experts)
     gate = jnp.sum(jnp.where(mine[None, :], parts, 0.0), axis=1, keepdims=True)
-    gate_part = jnp.dot(x, expert_gate[0], preferred_element_type=F32)
-    up_part = jnp.dot(x, expert_up[0], preferred_element_type=F32)
-    act = (jax.nn.silu(gate_part) * up_part).astype(BF16)
-    result = jnp.dot(act, expert_down[0], preferred_element_type=F32).astype(BF16)
-    weighted = (result.astype(F32) * gate).astype(BF16)
+    hidden = expert_gate.shape[2]
+    row_tile, tile = min(512, flat.shape[0]), min(256, hidden)
+    weighted = pl.pallas_call(
+        expert_kernel,
+        grid=(flat.shape[0] // row_tile, hidden // tile),
+        in_specs=[
+            pl.BlockSpec((row_tile, width + lanes), lambda r, i: (r, 0)),
+            pl.BlockSpec((width, tile), lambda r, i: (0, i)),
+            pl.BlockSpec((width, tile), lambda r, i: (0, i)),
+            pl.BlockSpec((tile, width), lambda r, i: (i, 0)),
+            pl.BlockSpec((row_tile, 1), lambda r, i: (r, 0)),
+        ],
+        out_specs=pl.BlockSpec((row_tile, width), lambda r, i: (r, 0)),
+        out_shape=jax.ShapeDtypeStruct((flat.shape[0], width), BF16),
+        scratch_shapes=[vmem((row_tile, width), F32)],
+        compiler_params=pltpu.CompilerParams(vmem_limit_bytes=VLIMIT),
+    )(flat, expert_gate[0], expert_up[0], expert_down[0], gate)
 
     half = width // 2
     out = call(

time: 192 us -> 189 us (0.984)
  matrix products: 23.9 us -> 0 us
  Pallas kernels: 155 us -> 176 us
    dot_general x2 -> x0, matrix products: 23.9 us -> none  [the longest x1 16.6 us: local(): jnp.dot(act, expert_down[0], preferred_element_type=F32).astype(BF16)]
    pallas_call x0 -> x1, Pallas kernels: none -> 20.7 us  [local(): pl.pallas_call(expert_kernel, grid=(flat.shape[0] // row_tile, hidden //...]
where the time goes in v2:
time: 189 us
  Pallas kernels  176 us (93%)
  local copies, waits for them, and re-layouts  7.59 us (4%)
  other arithmetic  5.09 us (3%)
    pallas_call x4, Pallas kernels, call(): pl.pallas_call(kernel, out_shape=outs, in_specs=[vmem] * len(ins), out_sp...  139 us
    pallas_call x1, Pallas kernels, local(): pl.pallas_call(expert_kernel, grid=(flat.shape[0] // row_tile, hidden //...  20.7 us
    pallas_call x1, Pallas kernels, local(): pl.pallas_call(functools.partial(prefix_kernel, group), grid=(KVH,), in_s...  10.1 us
    pallas_call x1, Pallas kernels, local(): pl.pallas_call(functools.partial(project_kernel, own_heads), grid=(width...  6.06 us

profile of v2, /device:TPU:0, one launch (start us, length us, event | category | flops | bytes accessed | tf_op | source)
XLA Modules:
  0.0 188.7 jit_solution(561727995445126179)
XLA Ops:
  0.0 0.8 copy.24
  0.8 0.1 convert_reduce_fusion
  0.9 0.7 select_maximum_fusion.chosen_ref
  1.5 1.6 pad_maximum_fusion.in_ref
  3.2 1.4 copy.22
  4.6 1.7 fusion.2.router_ref
  6.3 29.6 %shard_map.136 = bf16[4,2,16,5120]{3,2,1,0:T(8,128)(2,1)} custom-call(bf16[16,5120]{1,0:T(8,128)(2,1)} %pad_maximum_fusion.in_ref), custom_call_target="tpu_custom_call" | custom-call | tf_op jit(solution)/shard_map/pallas_call | solution.py:96
  35.9 1.4 constant_dynamic-slice_fusion
  37.3 1.6 constant_dynamic-slice_fusion.2.q_ref
  38.9 10.1 %shard_map.137 = (f32[4096,128]{1,0:T(8,128)}, f32[32,128]{1,0:T(8,128)}, f32[32,128]{1,0:T(8,128)}) custom-call(bf16[128,5120]{1,0:T(8,128)(2,1)} %bitcast.26, bf16[1024,512]{1,0:T(8,128)(2,1)} %bitcast.31, bf16[1024,512]{1,0:T(8,128)(2,1)} %bitcast.32), custom_call_target="tpu_custom_call" | custom-call | tf_op jit(solution)/shard_map/pallas_call | solution.py:491
  49.0 27.2 %shard_map.138 = (f32[512,128]{1,0:T(8,128)}, f32[4,128]{1,0:T(4,128)}, f32[4,128]{1,0:T(4,128)}) custom-call(f32[8,512,128]{2,1,0:T(8,128)} %bitcast.30, f32[8,4,128]{2,1,0:T(4,128)} %bitcast.37, f32[8,4,128]{2,1,0:T(4,128)} %bitcast.38), custom_call_target="tpu_custom_call" | custom-call | tf_op jit(solution)/shard_map/pallas_call | solution.py:96
  76.3 6.1 %shard_map.139 = bf16[128,4096]{1,0:T(8,128)(2,1)} custom-call(bf16[128,512]{1,0:T(8,128)(2,1)} %constant_dynamic-slice_fusion.2.q_ref, bf16[128,128]{1,0:T(8,128)(2,1)} %get-tuple-element.22.k_ref, bf16[128,128]{1,0:T(8,128)(2,1)} %get-tuple-element.21.v_ref, s32[1,128]{1,0:T(1,128)} %par_ref.1, f32[512,128]{1,0:T(8,128)} %get-tuple-element.16.o_ref, ...), custom_call_target="tpu_custom_call" | custom-call | tf_op jit(solution)/shard_map/pallas_call | solution.py:541
  82.3 47.0 %shard_map.140 = (f32[16,4096]{1,0:T(8,128)}, bf16[2,4,2,2,16,4224]{5,4,3,2,1,0:T(8,128)(2,1)}) custom-call(bf16[4,2,16,4096]{3,2,1,0:T(8,128)(2,1)} %bitcast.29, bf16[16,4096]{1,0:T(8,128)(2,1)} %bitcast.34, f32[1,4096]{1,0:T(1,128)} %bitcast.36, bf16[4096,128]{1,0:T(8,128)(2,1)} %fusion.2.router_ref, f32[16,128]{1,0:T(8,128)} %select_maximum_fusion.chosen_ref), custom_call_target="tpu_custom_call" | custom-call | tf_op jit(solution)/shard_map/pallas_call | solution.py:96
  129.4 1.0 select_reduce_fusion
  130.4 0.9 copy.25.gate_ref
  131.2 20.7 %shard_map.141 = bf16[512,4096]{1,0:T(8,128)(2,1)} custom-call(bf16[512,4224]{1,0:T(8,128)(2,1)} %bitcast.28, bf16[4096,768]{1,0:T(8,128)(2,1)} %bitcast.21, bf16[4096,768]{1,0:T(8,128)(2,1)} %bitcast.22, bf16[768,4096]{1,0:T(8,128)(2,1)} %bitcast.23, f32[512,1]{1,0:T(8,128)} %copy.25.gate_ref), custom_call_target="tpu_custom_call" | custom-call | tf_op jit(solution)/shard_map/pallas_call | solution.py:589
  152.0 35.1 %shard_map.142 = bf16[16,4096]{1,0:T(8,128)(2,1)} custom-call(bf16[2,4,2,2,16,4096]{5,4,3,2,1,0:T(8,128)(2,1)} %bitcast.20, f32[16,4096]{1,0:T(8,128)} %get-tuple-element.20.mixed_ref), custom_call_target="tpu_custom_call" | custom-call | tf_op jit(solution)/shard_map/pallas_call | solution.py:96
  187.1 1.6 copy.27
  (1 shorter events, 0.0 us)

commit v3 on v2

--- a/solution.py
+++ b/solution.py
@@ -585,7 +585,7 @@
     mine = (lane == expert) | (lane == expert + experts)
     gate = jnp.sum(jnp.where(mine[None, :], parts, 0.0), axis=1, keepdims=True)
     hidden = expert_gate.shape[2]
-    row_tile, tile = min(512, flat.shape[0]), min(256, hidden)
+    row_tile, tile = min(512, flat.shape[0]), min(384, hidden)
     weighted = pl.pallas_call(
         expert_kernel,
         grid=(flat.shape[0] // row_tile, hidden // tile),

time: 189 us -> 193 us (1.021)
  Pallas kernels: 176 us -> 179 us
    pallas_call x1, Pallas kernels: 20.7 us -> 24.2 us  [local(): pl.pallas_call(expert_kernel, grid=(flat.shape[0] // row_tile, hidden //...]
where the time goes in v3:
time: 193 us; the launch traced here: 192 us
  Pallas kernels  179 us (93%)
  local copies, waits for them, and re-layouts  7.59 us (4%)
  other arithmetic  5.09 us (3%)
    pallas_call x4, Pallas kernels, call(): pl.pallas_call(kernel, out_shape=outs, in_specs=[vmem] * len(ins), out_sp...  139 us
    pallas_call x1, Pallas kernels, local(): pl.pallas_call(expert_kernel, grid=(flat.shape[0] // row_tile, hidden //...  24.2 us
    pallas_call x1, Pallas kernels, local(): pl.pallas_call(functools.partial(prefix_kernel, group), grid=(KVH,), in_s...  10.1 us
    pallas_call x1, Pallas kernels, local(): pl.pallas_call(functools.partial(project_kernel, own_heads), grid=(width...  6.06 us

profile of v3, /device:TPU:0, one launch (start us, length us, event | category | flops | bytes accessed | tf_op | source)
XLA Modules:
  0.0 192.1 jit_solution(11605805826017901055)
XLA Ops:
  0.0 0.8 copy.24
  0.8 0.1 convert_reduce_fusion
  0.9 0.7 select_maximum_fusion.chosen_ref
  1.5 1.6 pad_maximum_fusion.in_ref
  3.2 1.4 copy.22
  4.6 1.7 fusion.2.router_ref
  6.3 29.6 %shard_map.136 = bf16[4,2,16,5120]{3,2,1,0:T(8,128)(2,1)} custom-call(bf16[16,5120]{1,0:T(8,128)(2,1)} %pad_maximum_fusion.in_ref), custom_call_target="tpu_custom_call" | custom-call | tf_op jit(solution)/shard_map/pallas_call | solution.py:96
  35.9 1.4 constant_dynamic-slice_fusion
  37.3 1.6 constant_dynamic-slice_fusion.2.q_ref
  38.9 10.1 %shard_map.137 = (f32[4096,128]{1,0:T(8,128)}, f32[32,128]{1,0:T(8,128)}, f32[32,128]{1,0:T(8,128)}) custom-call(bf16[128,5120]{1,0:T(8,128)(2,1)} %bitcast.26, bf16[1024,512]{1,0:T(8,128)(2,1)} %bitcast.31, bf16[1024,512]{1,0:T(8,128)(2,1)} %bitcast.32), custom_call_target="tpu_custom_call" | custom-call | tf_op jit(solution)/shard_map/pallas_call | solution.py:491
  49.0 27.2 %shard_map.138 = (f32[512,128]{1,0:T(8,128)}, f32[4,128]{1,0:T(4,128)}, f32[4,128]{1,0:T(4,128)}) custom-call(f32[8,512,128]{2,1,0:T(8,128)} %bitcast.30, f32[8,4,128]{2,1,0:T(4,128)} %bitcast.37, f32[8,4,128]{2,1,0:T(4,128)} %bitcast.38), custom_call_target="tpu_custom_call" | custom-call | tf_op jit(solution)/shard_map/pallas_call | solution.py:96
  76.3 6.1 %shard_map.139 = bf16[128,4096]{1,0:T(8,128)(2,1)} custom-call(bf16[128,512]{1,0:T(8,128)(2,1)} %constant_dynamic-slice_fusion.2.q_ref, bf16[128,128]{1,0:T(8,128)(2,1)} %get-tuple-element.22.k_ref, bf16[128,128]{1,0:T(8,128)(2,1)} %get-tuple-element.21.v_ref, s32[1,128]{1,0:T(1,128)} %par_ref.1, f32[512,128]{1,0:T(8,128)} %get-tuple-element.16.o_ref, ...), custom_call_target="tpu_custom_call" | custom-call | tf_op jit(solution)/shard_map/pallas_call | solution.py:541
  82.3 47.0 %shard_map.140 = (f32[16,4096]{1,0:T(8,128)}, bf16[2,4,2,2,16,4224]{5,4,3,2,1,0:T(8,128)(2,1)}) custom-call(bf16[4,2,16,4096]{3,2,1,0:T(8,128)(2,1)} %bitcast.29, bf16[16,4096]{1,0:T(8,128)(2,1)} %bitcast.34, f32[1,4096]{1,0:T(1,128)} %bitcast.36, bf16[4096,128]{1,0:T(8,128)(2,1)} %fusion.2.router_ref, f32[16,128]{1,0:T(8,128)} %select_maximum_fusion.chosen_ref), custom_call_target="tpu_custom_call" | custom-call | tf_op jit(solution)/shard_map/pallas_call | solution.py:96
  129.4 1.0 select_reduce_fusion
  130.4 0.9 copy.25.gate_ref
  131.2 24.2 %shard_map.141 = bf16[512,4096]{1,0:T(8,128)(2,1)} custom-call(bf16[512,4224]{1,0:T(8,128)(2,1)} %bitcast.28, bf16[4096,768]{1,0:T(8,128)(2,1)} %bitcast.21, bf16[4096,768]{1,0:T(8,128)(2,1)} %bitcast.22, bf16[768,4096]{1,0:T(8,128)(2,1)} %bitcast.23, f32[512,1]{1,0:T(8,128)} %copy.25.gate_ref), custom_call_target="tpu_custom_call" | custom-call | tf_op jit(solution)/shard_map/pallas_call | solution.py:589
  155.5 35.1 %shard_map.142 = bf16[16,4096]{1,0:T(8,128)(2,1)} custom-call(bf16[2,4,2,2,16,4096]{5,4,3,2,1,0:T(8,128)(2,1)} %bitcast.20, f32[16,4096]{1,0:T(8,128)} %get-tuple-element.20.mixed_ref), custom_call_target="tpu_custom_call" | custom-call | tf_op jit(solution)/shard_map/pallas_call | solution.py:96
  190.6 1.6 copy.27
  (1 shorter events, 0.0 us)

commit v4 on v2

--- a/solution.py
+++ b/solution.py
@@ -455,13 +455,14 @@
     def _():
         acc_ref[...] = part
 
-    @pl.when(i > 0)
+    @pl.when((i > 0) & (i < last))
     def _():
         acc_ref[...] += part
 
     @pl.when(i == last)
     def _():
-        out_ref[...] = (acc_ref[...].astype(BF16).astype(F32) * gate_ref[...]).astype(BF16)
+        total = jnp.where(i > 0, acc_ref[...] + part, part)
+        out_ref[...] = (total.astype(BF16).astype(F32) * gate_ref[...]).astype(BF16)
 
 
 def local(

time: 189 us -> 190 us (level)
  no operation moved by 1% of the time
where the time goes in v4:
time: 190 us; the launch traced here: 189 us
  Pallas kernels  176 us (93%)
  local copies, waits for them, and re-layouts  7.59 us (4%)
  other arithmetic  5.09 us (3%)
    pallas_call x4, Pallas kernels, call(): pl.pallas_call(kernel, out_shape=outs, in_specs=[vmem] * len(ins), out_sp...  139 us
    pallas_call x1, Pallas kernels, local(): pl.pallas_call(expert_kernel, grid=(flat.shape[0] // row_tile, hidden //...  21.1 us
    pallas_call x1, Pallas kernels, local(): pl.pallas_call(functools.partial(prefix_kernel, group), grid=(KVH,), in_s...  10.1 us
    pallas_call x1, Pallas kernels, local(): pl.pallas_call(functools.partial(project_kernel, own_heads), grid=(width...  6.06 us

profile of v4, /device:TPU:0, one launch (start us, length us, event | category | flops | bytes accessed | tf_op | source)
XLA Modules:
  0.0 189.1 jit_solution(14244047971930288459)
XLA Ops:
  0.0 0.8 copy.24
  0.8 0.1 convert_reduce_fusion
  0.9 0.7 select_maximum_fusion.chosen_ref
  1.5 1.6 pad_maximum_fusion.in_ref
  3.2 1.4 copy.22
  4.6 1.7 fusion.2.router_ref
  6.3 29.6 %shard_map.136 = bf16[4,2,16,5120]{3,2,1,0:T(8,128)(2,1)} custom-call(bf16[16,5120]{1,0:T(8,128)(2,1)} %pad_maximum_fusion.in_ref), custom_call_target="tpu_custom_call" | custom-call | tf_op jit(solution)/shard_map/pallas_call | solution.py:96
  35.9 1.4 constant_dynamic-slice_fusion
  37.3 1.6 constant_dynamic-slice_fusion.2.q_ref
  38.9 10.1 %shard_map.137 = (f32[4096,128]{1,0:T(8,128)}, f32[32,128]{1,0:T(8,128)}, f32[32,128]{1,0:T(8,128)}) custom-call(bf16[128,5120]{1,0:T(8,128)(2,1)} %bitcast.26, bf16[1024,512]{1,0:T(8,128)(2,1)} %bitcast.31, bf16[1024,512]{1,0:T(8,128)(2,1)} %bitcast.32), custom_call_target="tpu_custom_call" | custom-call | tf_op jit(solution)/shard_map/pallas_call | solution.py:492
  49.0 27.2 %shard_map.138 = (f32[512,128]{1,0:T(8,128)}, f32[4,128]{1,0:T(4,128)}, f32[4,128]{1,0:T(4,128)}) custom-call(f32[8,512,128]{2,1,0:T(8,128)} %bitcast.30, f32[8,4,128]{2,1,0:T(4,128)} %bitcast.37, f32[8,4,128]{2,1,0:T(4,128)} %bitcast.38), custom_call_target="tpu_custom_call" | custom-call | tf_op jit(solution)/shard_map/pallas_call | solution.py:96
  76.3 6.1 %shard_map.139 = bf16[128,4096]{1,0:T(8,128)(2,1)} custom-call(bf16[128,512]{1,0:T(8,128)(2,1)} %constant_dynamic-slice_fusion.2.q_ref, bf16[128,128]{1,0:T(8,128)(2,1)} %get-tuple-element.22.k_ref, bf16[128,128]{1,0:T(8,128)(2,1)} %get-tuple-element.21.v_ref, s32[1,128]{1,0:T(1,128)} %par_ref.1, f32[512,128]{1,0:T(8,128)} %get-tuple-element.16.o_ref, ...), custom_call_target="tpu_custom_call" | custom-call | tf_op jit(solution)/shard_map/pallas_call | solution.py:542
  82.3 47.0 %shard_map.140 = (f32[16,4096]{1,0:T(8,128)}, bf16[2,4,2,2,16,4224]{5,4,3,2,1,0:T(8,128)(2,1)}) custom-call(bf16[4,2,16,4096]{3,2,1,0:T(8,128)(2,1)} %bitcast.29, bf16[16,4096]{1,0:T(8,128)(2,1)} %bitcast.34, f32[1,4096]{1,0:T(1,128)} %bitcast.36, bf16[4096,128]{1,0:T(8,128)(2,1)} %fusion.2.router_ref, f32[16,128]{1,0:T(8,128)} %select_maximum_fusion.chosen_ref), custom_call_target="tpu_custom_call" | custom-call | tf_op jit(solution)/shard_map/pallas_call | solution.py:96
  129.4 1.0 select_reduce_fusion
  130.4 0.9 copy.25.gate_ref
  131.2 21.1 %shard_map.141 = bf16[512,4096]{1,0:T(8,128)(2,1)} custom-call(bf16[512,4224]{1,0:T(8,128)(2,1)} %bitcast.28, bf16[4096,768]{1,0:T(8,128)(2,1)} %bitcast.21, bf16[4096,768]{1,0:T(8,128)(2,1)} %bitcast.22, bf16[768,4096]{1,0:T(8,128)(2,1)} %bitcast.23, f32[512,1]{1,0:T(8,128)} %copy.25.gate_ref), custom_call_target="tpu_custom_call" | custom-call | tf_op jit(solution)/shard_map/pallas_call | solution.py:590
  152.4 35.1 %shard_map.142 = bf16[16,4096]{1,0:T(8,128)(2,1)} custom-call(bf16[2,4,2,2,16,4096]{5,4,3,2,1,0:T(8,128)(2,1)} %bitcast.20, f32[16,4096]{1,0:T(8,128)} %get-tuple-element.20.mixed_ref), custom_call_target="tpu_custom_call" | custom-call | tf_op jit(solution)/shard_map/pallas_call | solution.py:96
  187.5 1.6 copy.27
  (1 shorter events, 0.0 us)
